TPU v7x, 32 devices: a whole 2x2x4 slice. The times are simulated.
32 devices in a mesh: groups: 2 (over x), row: 16 (over z, y, core).
Axes of the slice: x: 2, y: 2, z: 4, core: 2. Of those that a mesh axis runs over, the one named last changes fastest.
Arguments:
- homolog_features: bfloat16 [256, 256, 256], P(('groups', 'row')), parts along dimension 0, may hold values from -6 to 6
- standardize_scale: float32 [256], replicated, may hold values from 0.25 to 1.75
- standardize_shift: float32 [256], replicated, may hold values from -3 to 3
- first_factor_matrix: bfloat16 [256, 32], replicated, may hold values from -0.375 to 0.375
- first_factor_intercept: float32 [32], replicated, may hold values from -3 to 3
- second_factor_matrix: bfloat16 [256, 32], replicated, may hold values from -0.375 to 0.375
- second_factor_intercept: float32 [32], replicated, may hold values from -3 to 3
- final_mapping_matrix: bfloat16 [1024, 128], replicated, may hold values from -2 to 2
- final_mapping_intercept: float32 [128], replicated, may hold values from -3 to 3
Outputs:
- pair: bfloat16 [512, 256, 128], P(('groups', 'row')), parts along dimension 0
There are 2 independent parts, one for each index of `groups`. A program takes and returns all parts, laid end to end along the dimension named above; an argument that names none is the same for every part. Nothing has to cross between parts.
All inputs are finite; a program needn't handle non-finite values.
Results may differ from a plain program's by a relative error of at most 0.0054.
Values may be sent and summed in bfloat16 or wider, within the bound.
A program may use at most 128 MiB of HBM per device.

v0:
```python
import jax
import jax.numpy as jnp
from jax import lax
from jax.sharding import PartitionSpec as P


def build_factor_pairs(
    homolog_features,
    standardize_scale,
    standardize_shift,
    first_factor_matrix,
    first_factor_intercept,
    second_factor_matrix,
    second_factor_intercept,
):
    element_quantities = homolog_features.astype(jnp.float32)
    average = jnp.mean(element_quantities, axis=-1, keepdims=True)
    centered = element_quantities - average
    variance = jnp.mean(centered * centered, axis=-1, keepdims=True)
    normed = (
        centered * lax.rsqrt(variance + 1e-05) * standardize_scale + standardize_shift
    ).astype(jnp.bfloat16)
    flattened = normed.reshape(-1, normed.shape[-1])
    first_factor_rows = (
        jnp.dot(flattened, first_factor_matrix, preferred_element_type=jnp.float32)
        + first_factor_intercept
    ).astype(jnp.bfloat16)
    second_factor_rows = (
        jnp.dot(flattened, second_factor_matrix, preferred_element_type=jnp.float32)
        + second_factor_intercept
    ).astype(jnp.bfloat16)
    tensor_shape_info = (
        homolog_features.shape[0],
        homolog_features.shape[1],
        first_factor_matrix.shape[1],
    )
    return (
        first_factor_rows.reshape(tensor_shape_info),
        second_factor_rows.reshape(tensor_shape_info),
    )


def pair_columns(first_factor_rows, columns, final_mapping_matrix, final_mapping_intercept):
    seq_count, row_count, width = first_factor_rows.shape
    col_count = columns.shape[1]
    block_cols = 128
    block_count = col_count // block_cols
    blocks = columns.reshape(seq_count, block_count, block_cols, width).transpose(1, 0, 2, 3)
    inverse = 1.0 / seq_count

    def single_block(block):
        outer = (
            jnp.einsum(
                "sic,sje->ijce", first_factor_rows, block, preferred_element_type=jnp.float32
            )
            * inverse
        )
        outer = outer.astype(jnp.bfloat16).reshape(row_count * block_cols, width * width)
        result = (
            jnp.dot(outer, final_mapping_matrix, preferred_element_type=jnp.float32)
            + final_mapping_intercept
        )
        return result.astype(jnp.bfloat16).reshape(
            row_count, block_cols, final_mapping_matrix.shape[1]
        )

    stacked = lax.map(single_block, blocks)
    return stacked.transpose(1, 0, 2, 3).reshape(
        row_count, col_count, final_mapping_matrix.shape[1]
    )


def local(
    homolog_features,
    standardize_scale,
    standardize_shift,
    first_factor_matrix,
    first_factor_intercept,
    second_factor_matrix,
    second_factor_intercept,
    final_mapping_matrix,
    final_mapping_intercept,
):
    partial_tensor_product = lax.all_to_all(
        homolog_features, "row", split_axis=1, concat_axis=0, tiled=True
    )
    first_factor_rows, second_factor_rows = build_factor_pairs(
        partial_tensor_product,
        standardize_scale,
        standardize_shift,
        first_factor_matrix,
        first_factor_intercept,
        second_factor_matrix,
        second_factor_intercept,
    )
    return pair_columns(
        first_factor_rows,
        lax.all_gather(second_factor_rows, "row", axis=1, tiled=True),
        final_mapping_matrix,
        final_mapping_intercept,
    )


def solution(mesh):
    in_specs = (P(("groups", "row"), None, None), P(), P(), P(), P(), P(), P(), P(), P())
    out_specs = P(("groups", "row"), None, None)
    return jax.shard_map(local, mesh=mesh, in_specs=in_specs, out_specs=out_specs, check_vma=False)
```

profile of v0, /device:TPU:0, one launch (start us, length us, event | category | flops | bytes accessed | tf_op | source)
XLA Modules:
  0.0 149.1 jit_solution(12805074621739112709)
XLA Ops:
  6.5 0.0 copy-start
  6.5 0.0 all-gather.2.cloned.1.call-start
  6.5 1.8 %copy.29 = bf16[8,256,256]{2,0,1:T(8,128)(2,1)S(1)} copy(bf16[8,256,256]{2,1,0:T(8,128)(2,1)} %param.11) | data formatting | bytes 2097152 | tf_op args[0]
  8.4 32.0 %all_to_all.4 = bf16[8,256,256]{2,0,1:T(8,128)(2,1)S(1)} all-to-all(bf16[8,256,256]{2,0,1:T(8,128)(2,1)S(1)} %copy.29), channel_id=1, replica_groups=mesh['groups'=2,'row'=16] {'row'}, dimensions={1} | all-to-all | bytes 2097152 | tf_op jit(solution)/shard_map/all_to_all | solution.py:84
  40.4 0.3 fusion.21
  40.7 0.3 fusion.20
  41.1 0.6 multiply_reduce_fusion
  41.8 0.1 rsqrt.12
  41.9 0.1 div.9
  42.0 0.0 copy-start.2
  42.0 0.0 copy-start.3
  42.0 0.2 copy.31
  42.2 0.5 copy-done.2
  42.6 0.0 copy-done.3
  42.7 0.0 copy-start.4
  42.7 0.0 copy-start.1
  42.7 0.0 copy-start.5
  42.7 0.9 fusion.19
  43.5 0.0 copy-done
  43.6 0.0 copy-done.4
  43.6 0.4 fusion.14
  44.0 1.0 copy.34
  45.0 0.0 all-gather.2.cloned.1.call-update
  45.0 0.0 copy-done.1
  45.0 0.0 copy-done.5
  45.0 0.4 fusion.15
  45.5 0.3 copy.36
  45.7 0.4 copy.38
  46.2 77.4 %all-gather.2.cloned.1.call-done = bf16[128,256,32]{2,1,0:T(8,128)(2,1)} async-done(((bf16[128,16,32]{2,1,0:T(8,128)(2,1)}), bf16[128,256,32]{2,1,0:T(8,128)(2,1)}) %all-gather.2.cloned.1.call-update) | async-done | bytes 2097168 | tf_op jit(solution)/shard_map/all_gather | solution.py:98
  123.6 0.0 copy-start.6
  123.6 7.7 %copy.37 = bf16[2,128,128,32]{2,1,3,0:T(8,128)(2,1)S(1)} copy(bf16[2,128,128,32]{3,2,0,1:T(8,128)(2,1)} %bitcast.72) | data formatting | bytes 4194304 | tf_op jit(solution)/shard_map/while | solution.py:67
  131.2 0.0 copy-done.6
  131.2 9.9 %while.10 = (s32[]{:T(128)}, bf16[2,16,128,128]{3,2,1,0:T(8,128)(2,1)S(1)}, bf16[2,128,128,32]{2,1,3,0:T(8,128)(2,1)S(1)}, bf16[128,16,32]{0,2,1:T(8,128)(2,1)S(...) while((s32[]{:T(128)}, bf16[2,16,128,128]{3,2,1,0:T(8,128)(2,1)S(1)}, ...), condition=%wide.region_3.4_spmd, body=%wide.region_2.3_spmd.sunk | while | flops 1078460416 | bytes 19794544 | solution.py:67
  131.3 1.2 fusion.37
  132.5 0.0 copy-start.7
  132.5 1.6 %copy.56 = bf16[16,128,32,32]{1,0,3,2:T(8,128)(2,1)S(1)} copy(bf16[16,128,32,32]{1,2,0,3:T(8,128)(2,1)S(1)} %fusion.37) | data formatting | bytes 8388608 | tf_op jit(solution)/shard_map/while/body/eval_jaxpr/convert_element_type | solution.py:58
  134.1 0.0 copy-done.7
  134.2 2.0 %fusion.38 = bf16[2048,128]{1,0:T(8,128)(2,1)S(1)} fusion(bf16[1024,128]{1,0:T(8,128)(2,1)S(1)} %get-tuple-element.131, bf16[128,8,16,128]{3,2,1,0:T(8,128)(2,1)S(1)} %bitcast.68, f32[128]{0:T(128)S(1)} %copy-done.7), kind=kOutput, calls=%fused_computation.6.clone.1 | convolution fusion | flops 537395200 | bytes 4981248 | tf_op jit(solution)/shard_map/while/body/eval_jaxpr/dot_general | solution.py:60
  136.1 0.1 constant_dynamic-update-slice_fusion.2
  136.2 1.2 fusion.37
  137.5 0.0 copy-start.7
  137.5 1.6 %copy.56 = bf16[16,128,32,32]{1,0,3,2:T(8,128)(2,1)S(1)} copy(bf16[16,128,32,32]{1,2,0,3:T(8,128)(2,1)S(1)} %fusion.37) | data formatting | bytes 8388608 | tf_op jit(solution)/shard_map/while/body/eval_jaxpr/convert_element_type | solution.py:58
  139.1 0.0 copy-done.7
  139.1 2.0 %fusion.38 = bf16[2048,128]{1,0:T(8,128)(2,1)S(1)} fusion(bf16[1024,128]{1,0:T(8,128)(2,1)S(1)} %get-tuple-element.131, bf16[128,8,16,128]{3,2,1,0:T(8,128)(2,1)S(1)} %bitcast.68, f32[128]{0:T(128)S(1)} %copy-done.7), kind=kOutput, calls=%fused_computation.6.clone.1 | convolution fusion | flops 537395200 | bytes 4981248 | tf_op jit(solution)/shard_map/while/body/eval_jaxpr/dot_general | solution.py:60
  141.1 0.1 constant_dynamic-update-slice_fusion.2
  141.2 1.0 copy.39
  (5 shorter events, 0.1 us)
Async XLA Ops:
  6.5 37.0 %copy-start = (bf16[256,32]{0,1:T(8,128)(2,1)S(1)}, bf16[256,32]{0,1:T(8,128)(2,1)}, u32[]{:S(2)}) copy-start(bf16[256,32]{0,1:T(8,128)(2,1)} %param.16) | copy-start | bytes 49156
  6.5 117.0 %all-gather.2.cloned.1.call-start = ((), (), s32[]{:S(2)}) async-start(), calls=%async_computation.1 | async-start | bytes 8912896 | tf_op jit(solution)/shard_map/all_gather | solution.py:98
  42.0 0.7 copy-start.2
  42.0 0.7 copy-start.3
  42.7 0.9 copy-start.4
  42.7 2.4 %copy-start.1 = (bf16[256,32]{0,1:T(8,128)(2,1)S(1)}, bf16[256,32]{0,1:T(8,128)(2,1)}, u32[]{:S(2)}) copy-start(bf16[256,32]{0,1:T(8,128)(2,1)} %param.14) | copy-start | bytes 49156
  42.7 2.4 %copy-start.5 = (f32[32]{0:T(128)S(1)}, f32[32]{0:T(128)}, u32[]{:S(2)}) copy-start(f32[32]{0:T(128)} %param.15) | copy-start | bytes 388
  123.6 7.7 %copy-start.6 = (bf16[1024,128]{1,0:T(8,128)(2,1)S(1)}, bf16[1024,128]{1,0:T(8,128)(2,1)}, u32[]{:S(2)}) copy-start(bf16[1024,128]{1,0:T(8,128)(2,1)} %param.18) | copy-start | bytes 786436
  132.5 1.6 %copy-start.7 = (f32[128]{0:T(128)S(1)}, f32[128]{0:T(128)}, u32[]{:S(2)}) copy-start(f32[128]{0:T(128)} %get-tuple-element.132) | copy-start | bytes 1540 | tf_op jit(solution)/shard_map/while
  137.5 1.6 %copy-start.7 = (f32[128]{0:T(128)S(1)}, f32[128]{0:T(128)}, u32[]{:S(2)}) copy-start(f32[128]{0:T(128)} %get-tuple-element.132) | copy-start | bytes 1540 | tf_op jit(solution)/shard_map/while
Sparse Core Ops, SparseCore 0:
  45.1 78.3 all-gather.1
where the time goes:
time: 149 us
  waiting for transfers between devices  77.4 us (52%)
  blocking collectives  32 us (21%)
  local copies, waits for them, and re-layouts  16.6 us (11%)
  between operations  13.6 us (9%)
  matrix products  7.22 us (5%)
  other arithmetic  2.18 us (1%)
    all_gather x1, waiting for transfers between devices, local(): lax.all_gather(second_factor_rows, 'row', axis=1, tiled=True)  77.4 us
    all_to_all x1, blocking collectives, local(): lax.all_to_all(homolog_features, 'row', split_axis=1, concat_axis=0, tile...  32 us
    while x2, local copies, waits for them, and re-layouts, pair_columns(): stacked = lax.map(single_block, blocks)  8.1 us
    dot_general x2, matrix products, single_block(): jnp.dot(outer, final_mapping_matrix, preferred_element_type=jnp.float32)  3.93 us
    convert_element_type x2, local copies, waits for them, and re-layouts, single_block(): outer.astype(jnp.bfloat16).reshape(row_count * block_cols, width * width)  3.24 us
  transfers between devices with their start and end apart: 1, of which 1 were waited for; matrix products, arithmetic and copies ran while one was open for 1% of the time, Pallas kernels for 0%

commit v1 on v0

v1 whole, which is shorter than its diff:
```python
import functools

import jax
import jax.numpy as jnp
from jax import lax
from jax.experimental import pallas as pl
from jax.experimental.pallas import tpu as pltpu
from jax.sharding import PartitionSpec as P

LANES = 128
ROWS16 = 16


class Sizes:
    def __init__(self, n, seqs, residues, width, cz):
        self.n = n
        self.seqs = seqs
        self.res = residues
        self.width = width
        self.cz = cz
        self.own = residues // n
        self.parts = ROWS16 // seqs
        self.eper = width // self.parts
        self.chunks = residues // LANES
        self.tiles = self.chunks * self.eper
        self.pack = LANES // width
        self.groups = self.own // self.pack
        self.ghigh = min(self.parts, self.groups)
        self.q = self.groups // self.ghigh
        self.k = n * ROWS16


def project(z, x_ref, scale_ref, shift_ref, w1_ref, b1_ref, w2_ref, b2_ref, wide, tall):
    w1 = jnp.concatenate([w1_ref[...]] * z.pack, axis=1)
    b1 = jnp.concatenate([b1_ref[...]] * z.pack, axis=1)
    w2t = w2_ref[...].astype(jnp.float32).T.astype(jnp.bfloat16)
    eye = lax.broadcasted_iota(jnp.int32, (z.width, z.width), 0) == lax.broadcasted_iota(
        jnp.int32, (z.width, z.width), 1
    )
    b2 = jnp.sum(jnp.where(eye, b2_ref[...], 0.0), axis=1, keepdims=True)
    scale = scale_ref[...]
    shift = shift_ref[...]
    for s in range(z.seqs):
        x = x_ref[s].astype(jnp.float32)
        average = jnp.mean(x, axis=-1, keepdims=True)
        centered = x - average
        variance = jnp.mean(centered * centered, axis=-1, keepdims=True)
        normed = (centered * lax.rsqrt(variance + 1e-05) * scale + shift).astype(jnp.bfloat16)
        tall[pl.ds(s * z.res, z.res), :] = (
            jnp.dot(normed, w1, preferred_element_type=jnp.float32) + b1
        )
        right = (
            lax.dot_general(
                w2t, normed, (((1,), (1,)), ((), ())), preferred_element_type=jnp.float32
            )
            + b2
        )
        for h in range(z.parts):
            for c in range(z.chunks):
                wide[pl.ds(c * z.eper * ROWS16 + h * z.seqs + s, z.eper, stride=ROWS16), :] = right[
                    h * z.eper : (h + 1) * z.eper, c * LANES : (c + 1) * LANES
                ]


def pack_left(z, tall, flat, block_ref):
    if z.ghigh * z.seqs < ROWS16:
        flat[...] = jnp.zeros_like(flat)
    lane = lax.broadcasted_iota(jnp.int32, (z.seqs, LANES), 1) // z.width
    for r in range(z.n):
        for g in range(z.groups):
            first = r * z.own + g * z.pack
            value = tall[pl.ds(first, z.seqs, stride=z.res), :]
            for p in range(1, z.pack):
                value = jnp.where(lane == p, tall[pl.ds(first + p, z.seqs, stride=z.res), :], value)
            q, gh = g // z.ghigh, g % z.ghigh
            flat[pl.ds((r * z.q + q) * ROWS16 + gh * z.seqs, z.seqs), :] = value
    block_ref[...] = flat[...].reshape(block_ref.shape).astype(jnp.bfloat16)


def spread_left(z, left_ref, a_ref):
    for q in range(z.q):
        block = left_ref[:, q].reshape(z.k, LANES).astype(jnp.float32).T
        part = (lax.broadcasted_iota(jnp.int32, block.shape, 1) // z.seqs) % z.parts
        for gh in range(z.ghigh):
            for h in range(z.parts):
                turn = ((h - gh) * z.seqs) % z.k
                moved = pltpu.roll(block, turn, 1) if turn else block
                first = h * z.own * z.width + (q * z.ghigh + gh) * LANES
                a_ref[pl.ds(first, LANES), :] = jnp.where(part == h, moved, 0.0).astype(jnp.bfloat16)


def turn_weights(z, w_ref, wide, wt_ref):
    wide[...] = w_ref[...].astype(jnp.float32)
    for e in range(z.width):
        rows = wide[pl.ds(e, z.width, stride=z.width), :]
        if e % z.pack == 0:
            held = []
        held.append(rows)
        if e % z.pack == z.pack - 1:
            first = (e - z.pack + 1) * z.width
            wt_ref[:, first : first + LANES] = jnp.concatenate(held, axis=0).T.astype(jnp.bfloat16)


def outer_chunk(z, c, a_ref, gathered, held):
    def body(pair, carry):
        tile = c * z.eper + 2 * pair
        b = jnp.concatenate(
            [gathered[:, tile + t].reshape(z.k, LANES) for t in range(2)], axis=1
        )
        for h in range(z.parts):
            o = jnp.dot(
                a_ref[pl.ds(h * z.own * z.width, z.own * z.width), :],
                b,
                preferred_element_type=jnp.float32,
            ).astype(jnp.bfloat16)
            for t in range(2):
                first = pl.multiple_of((h * z.eper + 2 * pair + t) * z.width, z.width)
                for i in range(z.own):
                    held[i // 2, pl.ds(first, z.width), pl.ds((i % 2) * LANES, LANES)] = o[
                        i * z.width : (i + 1) * z.width, t * LANES : (t + 1) * LANES
                    ]
        return carry

    lax.fori_loop(0, z.eper // 2, body, 0)


def map_chunk(z, c, inverse, wt_ref, bias_ref, held, out_ref):
    bias = bias_ref[...]

    def body(pair, carry):
        result = jnp.dot(wt_ref[...], held[pair], preferred_element_type=jnp.float32)
        for t in range(2):
            value = result[:, t * LANES : (t + 1) * LANES].T * inverse + bias
            out_ref[2 * pair + t, pl.ds(c * LANES, LANES), :] = value.astype(jnp.bfloat16)
        return carry

    lax.fori_loop(0, z.own // 2, body, 0)


def project_kernel(z, x, scale, shift, w1, b1, w2, b2, right_ref, left_ref, wide, tall, flat):
    project(z, x, scale, shift, w1, b1, w2, b2, wide, tall)
    right_ref[...] = wide[...].reshape(right_ref.shape).astype(jnp.bfloat16)
    pack_left(z, tall, flat, left_ref)


def pair_kernel(z, inverse, gathered, left, w, bias, out_ref, wide, wt, a, held):
    turn_weights(z, w, wide, wt)
    spread_left(z, left, a)
    for c in range(z.chunks):
        outer_chunk(z, c, a, gathered, held)
        map_chunk(z, c, inverse, wt, bias, held, out_ref)


def solution(mesh):
    n = mesh.shape["row"]
    vmem = pl.BlockSpec(memory_space=pltpu.VMEM)

    def local(x, scale, shift, w1, b1, w2, b2, w, bias):
        z = Sizes(n, x.shape[0], x.shape[1], w1.shape[1], w.shape[1])
        inverse = 1.0 / (n * x.shape[0])
        right, left = pl.pallas_call(
            functools.partial(project_kernel, z),
            out_shape=(
                jax.ShapeDtypeStruct((z.tiles, ROWS16, LANES), jnp.bfloat16),
                jax.ShapeDtypeStruct((n, z.q, ROWS16, LANES), jnp.bfloat16),
            ),
            in_specs=[vmem] * 7,
            out_specs=(vmem, vmem),
            scratch_shapes=[
                pltpu.VMEM((z.tiles * ROWS16, LANES), jnp.float32),
                pltpu.VMEM((z.seqs * z.res, LANES), jnp.float32),
                pltpu.VMEM((n * z.q * ROWS16, LANES), jnp.float32),
            ],
            compiler_params=pltpu.CompilerParams(vmem_limit_bytes=48 * 2**20),
        )(x, scale.reshape(1, -1), shift.reshape(1, -1), w1, b1.reshape(1, -1), w2, b2.reshape(1, -1))
        left = lax.all_to_all(left, "row", split_axis=0, concat_axis=0, tiled=True)
        gathered = lax.all_gather(right, "row", axis=0, tiled=False)
        return pl.pallas_call(
            functools.partial(pair_kernel, z, inverse),
            out_shape=jax.ShapeDtypeStruct((z.own, z.res, z.cz), jnp.bfloat16),
            in_specs=[vmem] * 4,
            out_specs=vmem,
            scratch_shapes=[
                pltpu.VMEM(w.shape, jnp.float32),
                pltpu.VMEM((z.cz, w.shape[0]), jnp.bfloat16),
                pltpu.VMEM((z.parts * z.own * z.width, z.k), jnp.bfloat16),
                pltpu.VMEM((z.own // 2, z.width * z.width, 2 * LANES), jnp.bfloat16),
            ],
            compiler_params=pltpu.CompilerParams(vmem_limit_bytes=56 * 2**20),
        )(gathered, left, w, bias.reshape(1, -1))

    in_specs = (P(("groups", "row"), None, None), P(), P(), P(), P(), P(), P(), P(), P())
    return jax.shard_map(
        local,
        mesh=mesh,
        in_specs=in_specs,
        out_specs=P(("groups", "row"), None, None),
        check_vma=False,
    )
```

time: 149 us -> 80.1 us (0.54)
  waiting for transfers between devices: 77.4 us -> 29 us
  blocking collectives: 32 us -> 15.2 us
  Pallas kernels: 0 us -> 16.5 us
  local copies, waits for them, and re-layouts: 16.6 us -> 5.56 us
  matrix products: 7.22 us -> 0 us
  other arithmetic: 2.18 us -> 0 us
    all_gather x1, waiting for transfers between devices: 77.4 us -> 29 us  [local(): gathered = lax.all_gather(right, 'row', axis=0, tiled=False)]
    all_to_all x1, blocking collectives: 32 us -> 15.2 us  [local(): left = lax.all_to_all(left, 'row', split_axis=0, concat_axis=0, tiled=True)]
    pallas_call x0 -> x2, Pallas kernels: none -> 16.5 us  [the longest x1 13.9 us: local(): pl.pallas_call(functools.partial(pair_kernel, z, inverse), out_shape=jax....]
    while x6 -> x0, local copies, waits for them, and re-layouts: 8.11 us -> none  [the longest x2 8.1 us: pair_columns(): stacked = lax.map(single_block, blocks)]
    dot_general x6 -> x0, matrix products: 7.22 us -> none  [the longest x2 3.93 us: single_block(): jnp.dot(outer, final_mapping_matrix, preferred_element_type=jnp.float32)]
    convert_element_type x5 -> x0, local copies, waits for them, and re-layouts: 4.71 us -> none  [the longest x2 3.24 us: single_block(): outer.astype(jnp.bfloat16).reshape(row_count * block_cols, width * width)]
    unnamed x15 -> x12, local copies, waits for them, and re-layouts: 2.34 us -> 5.56 us
  transfers between devices with their start and end apart: 1 -> 1, of which waited for: 1 -> 1; matrix products, arithmetic and copies ran while one was open for 1% -> 0% of each run, Pallas kernels for 0% -> 0%
where the time goes in v1:
time: 80.1 us; the launch traced here: 79.7 us
  waiting for transfers between devices  29 us (36%)
  Pallas kernels  16.5 us (21%)
  blocking collectives  15.2 us (19%)
  between operations  13.4 us (17%)
  local copies, waits for them, and re-layouts  5.56 us (7%)
    all_gather x1, waiting for transfers between devices, local(): gathered = lax.all_gather(right, 'row', axis=0, tiled=False)  29 us
    all_to_all x1, blocking collectives, local(): left = lax.all_to_all(left, 'row', split_axis=0, concat_axis=0, tiled=True)  15.2 us
    pallas_call x1, Pallas kernels, local(): pl.pallas_call(functools.partial(pair_kernel, z, inverse), out_shape=jax....  13.9 us
    unnamed x12, local copies, waits for them, and re-layouts  5.56 us
    pallas_call x1, Pallas kernels, local(): pl.pallas_call(functools.partial(project_kernel, z), out_shape=(jax.Shape...  2.65 us
  transfers between devices with their start and end apart: 1, of which 1 were waited for; matrix products, arithmetic and copies ran while one was open for 0% of the time, Pallas kernels for 0%

profile of v1, /device:TPU:0, one launch (start us, length us, event | category | flops | bytes accessed | tf_op | source)
XLA Modules:
  0.0 79.7 jit_solution(18032456778567747478)
XLA Ops:
  6.5 0.0 all-gather.3.cloned.1.call-start
  6.5 0.8 %copy.12.w1 = bf16[256,32]{1,0:T(8,128)(2,1)S(1)} copy(bf16[256,32]{0,1:T(8,128)(2,1)} %param.12) | data formatting | bytes 32768 | tf_op args[3]
  7.4 0.8 %copy.13.w2 = bf16[256,32]{1,0:T(8,128)(2,1)S(1)} copy(bf16[256,32]{0,1:T(8,128)(2,1)} %param.14) | data formatting | bytes 32768 | tf_op args[5]
  8.2 0.0 copy-start
  8.2 1.2 %copy-done = bf16[8,256,256]{2,1,0:T(8,128)(2,1)S(1)} copy-done((bf16[8,256,256]{2,1,0:T(8,128)(2,1)S(1)}, bf16[8,256,256]{2,1,0:T(8,128)(2,1)}, u32[]{:S(2)}) %copy-start) | copy-done | bytes 1048600
  9.4 0.0 copy-start.1
  9.4 0.7 copy-done.1
  10.1 0.0 copy-start.2
  10.1 0.7 copy-done.2
  10.8 0.0 copy-start.3
  10.8 0.7 copy-done.3
  11.5 0.0 copy-start.4
  11.5 0.7 copy-done.4
  12.1 2.6 %shard_map.91 = (bf16[32,16,128]{2,1,0:T(8,128)(2,1)}, bf16[16,2,16,128]{3,2,1,0:T(8,128)(2,1)S(1)}) custom-call(bf16[8,256,256]{2,1,0:T(8,128)(2,1)S(1)} %copy-done, f32[1,256]{1,0:T(1,128)S(1)} %bitcast.6, f32[1,256]{1,0:T(1,128)S(1)} %bitcast.7, bf16[256,32]{1,0:T(8,128)(2,1)S(1)} %copy.12.w1, f32[1,32]{1,0:T(1,128)S(1)} %bitcast.8, ...), custom_call_target="tpu_custom_call" | custom-call | tf_op jit(solution)/shard_map/pallas_call | solution.py:161
  14.8 0.0 all-gather.3.cloned.1.call-update
  14.8 15.2 %all_to_all.5.left = bf16[16,2,16,128]{3,2,1,0:T(8,128)(2,1)} all-to-all(bf16[16,2,16,128]{3,2,1,0:T(8,128)(2,1)S(1)} %get-tuple-element.8), channel_id=1, replica_groups=mesh['groups'=2,'row'=16] {'row'}, dimensions={0} | all-to-all | bytes 262144 | tf_op jit(solution)/shard_map/all_to_all | solution.py:176
  30.0 29.0 %all-gather.3.cloned.1.call-done = bf16[512,16,128]{2,1,0:T(8,128)(2,1)} async-done(((bf16[32,16,128]{2,1,0:T(8,128)(2,1)}), bf16[512,16,128]{2,1,0:T(8,128)(2,1)}) %all-gather.3.cloned.1.call-update) | async-done | bytes 2097168 | tf_op jit(solution)/shard_map/all_gather | solution.py:177
  59.0 13.9 %shard_map.92 = bf16[16,256,128]{2,1,0:T(8,128)(2,1)} custom-call(bf16[16,32,16,128]{3,2,1,0:T(8,128)(2,1)} %bitcast.10, bf16[16,2,16,128]{3,2,1,0:T(8,128)(2,1)} %all_to_all.5.left, bf16[1024,128]{1,0:T(8,128)(2,1)} %w.1, f32[1,128]{1,0:T(1,128)} %bitcast.11), custom_call_target="tpu_custom_call" | custom-call | tf_op jit(solution)/shard_map/pallas_call | solution.py:178
Async XLA Ops:
  6.5 52.5 %all-gather.3.cloned.1.call-start = ((), (), s32[]{:S(2)}) async-start(), calls=%async_computation.1 | async-start | bytes 2228224 | tf_op jit(solution)/shard_map/all_gather | solution.py:177
  8.2 1.2 %copy-start = (bf16[8,256,256]{2,1,0:T(8,128)(2,1)S(1)}, bf16[8,256,256]{2,1,0:T(8,128)(2,1)}, u32[]{:S(2)}) copy-start(bf16[8,256,256]{2,1,0:T(8,128)(2,1)} %x.1) | copy-start | bytes 3145732
  9.4 0.7 copy-start.1
  10.1 0.7 copy-start.2
  10.8 0.7 copy-start.3
  11.5 0.7 copy-start.4
Sparse Core Ops, SparseCore 0:
  14.9 44.0 all-gather.2

commit v2 on v1

v2 whole, which is shorter than its diff:
```python
import functools

import jax
import jax.numpy as jnp
from jax import lax
from jax.experimental import pallas as pl
from jax.experimental.pallas import tpu as pltpu
from jax.sharding import PartitionSpec as P

LANES = 128
ROWS16 = 16
CONTRACT_LAST = (((1,), (1,)), ((), ()))
MESH = pl.DeviceIdType.MESH


class Sizes:
    def __init__(self, n, seqs, residues, width, cz):
        self.n = n
        self.seqs = seqs
        self.res = residues
        self.width = width
        self.cz = cz
        self.own = residues // n
        self.parts = ROWS16 // seqs
        self.eper = width // self.parts
        self.chunks = residues // LANES
        self.tiles = self.chunks * self.eper
        self.pack = LANES // width
        self.groups = self.own // self.pack
        self.ghigh = min(self.parts, self.groups)
        self.q = self.groups // self.ghigh
        self.k = n * ROWS16
        self.half = self.eper // 2
        self.waves = min(2, self.chunks)
        self.per_wave = self.chunks // self.waves
        self.piece = self.per_wave * self.half
        self.chips = n // 2
        self.hops = self.chips // 2

    def tile(self, chunk, u):
        wave, at = divmod(chunk, self.per_wave)
        return ((wave * 2 + u) * self.per_wave + at) * self.half


def project(z, wave, x_ref, params, wide, tall):
    w1, b1, w2, b2, scale, shift = params
    count = z.per_wave * LANES
    for s in range(z.seqs):
        x = x_ref[s, wave * count : (wave + 1) * count, :].astype(jnp.float32)
        average = jnp.mean(x, axis=-1, keepdims=True)
        centered = x - average
        variance = jnp.mean(centered * centered, axis=-1, keepdims=True)
        normed = (centered * lax.rsqrt(variance + 1e-05) * scale + shift).astype(jnp.bfloat16)
        tall[pl.ds(s * z.res + wave * count, count), :] = (
            lax.dot_general(normed, w1, CONTRACT_LAST, preferred_element_type=jnp.float32) + b1
        )
        right = (
            lax.dot_general(w2, normed, CONTRACT_LAST, preferred_element_type=jnp.float32) + b2
        )
        for h in range(z.parts):
            for at in range(z.per_wave):
                for u in range(2):
                    row = z.tile(wave * z.per_wave + at, u) * ROWS16 + h * z.seqs + s
                    first = h * z.eper + u * z.half
                    wide[pl.ds(row, z.half, stride=ROWS16), :] = right[
                        first : first + z.half, at * LANES : (at + 1) * LANES
                    ]


def pack_left(z, tall, flat, block_ref):
    if z.ghigh * z.seqs < ROWS16:
        flat[...] = jnp.zeros_like(flat)
    lane = lax.broadcasted_iota(jnp.int32, (z.seqs, LANES), 1) // z.width
    for r in range(z.n):
        for g in range(z.groups):
            first = r * z.own + g * z.pack
            value = tall[pl.ds(first, z.seqs, stride=z.res), :]
            for p in range(1, z.pack):
                value = jnp.where(lane == p, tall[pl.ds(first + p, z.seqs, stride=z.res), :], value)
            q, gh = g // z.ghigh, g % z.ghigh
            flat[pl.ds((r * z.q + q) * ROWS16 + gh * z.seqs, z.seqs), :] = value
    block_ref[...] = flat[...].reshape(block_ref.shape).astype(jnp.bfloat16)


def spread_left(z, left_ref, a_ref):
    for q in range(z.q):
        block = left_ref[:, q].reshape(z.k, LANES).astype(jnp.float32).T
        part = (lax.broadcasted_iota(jnp.int32, block.shape, 1) // z.seqs) % z.parts
        for gh in range(z.ghigh):
            for h in range(z.parts):
                turn = ((h - gh) * z.seqs) % z.k
                moved = pltpu.roll(block, turn, 1) if turn else block
                first = h * z.own * z.width + (q * z.ghigh + gh) * LANES
                a_ref[pl.ds(first, LANES), :] = jnp.where(part == h, moved, 0.0).astype(jnp.bfloat16)


def turn_weights(z, w_ref, wide, wt_ref):
    wide[...] = w_ref[...].astype(jnp.float32)
    for e in range(z.width):
        rows = wide[pl.ds(e, z.width, stride=z.width), :]
        if e % z.pack == 0:
            held = []
        held.append(rows)
        if e % z.pack == z.pack - 1:
            first = (e - z.pack + 1) * z.width
            wt_ref[:, first : first + LANES] = jnp.concatenate(held, axis=0).T.astype(jnp.bfloat16)


def outer_part(z, c, u, a_ref, gathered, held):
    def body(pair, carry):
        tile = z.tile(c, u) + 2 * pair
        b = jnp.concatenate(
            [gathered[:, tile + t].reshape(z.k, LANES) for t in range(2)], axis=1
        )
        for h in range(z.parts):
            o = jnp.dot(
                a_ref[pl.ds(h * z.own * z.width, z.own * z.width), :],
                b,
                preferred_element_type=jnp.float32,
            ).astype(jnp.bfloat16)
            for t in range(2):
                first = pl.multiple_of(
                    (h * z.eper + u * z.half + 2 * pair + t) * z.width, z.width
                )
                for i in range(z.own):
                    held[i // 2, pl.ds(first, z.width), pl.ds((i % 2) * LANES, LANES)] = o[
                        i * z.width : (i + 1) * z.width, t * LANES : (t + 1) * LANES
                    ]
        return carry

    lax.fori_loop(0, z.half // 2, body, 0)


def map_part(z, c, u, inverse, wt_ref, bias_ref, held, out_ref):
    bias = bias_ref[...]

    def body(pair, carry):
        result = jnp.dot(wt_ref[...], held[pair], preferred_element_type=jnp.float32)
        for t in range(2):
            value = result[:, t * LANES : (t + 1) * LANES].T * inverse + bias
            out_ref[2 * pair + t, pl.ds(c * LANES, LANES), :] = value.astype(jnp.bfloat16)
        return carry

    pairs = z.own // 2
    lax.fori_loop(u * pairs // 2, (u + 1) * pairs // 2, body, 0)


def kernel(z, inverse, *refs):
    hbm, out_ref = refs[:9], refs[9]
    local_refs = refs[10:19]
    wide, tall, flat, packed, left, gathered, wide_w, wt, a, held = refs[19:29]
    load_sem, ring_send, ring_recv, sib_send, sib_recv, left_send, left_recv = refs[29:]
    x, scale, shift, w1, b1, w2, b2, w, bias = local_refs

    me = lax.axis_index("row")
    core, chip = lax.rem(me, 2), me // 2
    place = jnp.where(lax.rem(chip, 2) == 0, chip // 2, z.chips - 1 - chip // 2)

    def device_at(p):
        p = lax.rem(p + z.chips, z.chips)
        at = jnp.where(p < z.chips // 2, 2 * p, 2 * (z.chips - 1 - p) + 1)
        return at * 2 + core

    ahead, behind, sibling = device_at(place + 1), device_at(place - 1), me + 1 - 2 * core

    loads = [
        pltpu.make_async_copy(hbm[k], local_refs[k], load_sem.at[k]) for k in range(1, 9)
    ]
    count = z.per_wave * LANES
    x_loads = [
        pltpu.make_async_copy(
            hbm[0].at[:, pl.ds(v * count, count)],
            x.at[:, pl.ds(v * count, count)],
            load_sem.at[9 + v],
        )
        for v in range(z.waves)
    ]
    x_loads[0].start()
    for load in loads:
        load.start()
    for load in x_loads[1:]:
        load.start()
    barrier = pltpu.get_barrier_semaphore()
    for k in range(1, z.n):
        pl.semaphore_signal(
            barrier, inc=1, device_id={"row": lax.rem(me + k, z.n)}, device_id_type=MESH
        )

    def ring(direction, hop, p, source):
        part = gathered.at[source, pl.ds(p * z.piece, z.piece)]
        return pltpu.make_async_remote_copy(
            src_ref=part,
            dst_ref=part,
            send_sem=ring_send.at[direction, hop - 1, p],
            recv_sem=ring_recv.at[direction, hop - 1, p],
            device_id={"row": (ahead, behind)[direction]},
            device_id_type=MESH,
        )

    def across(key, p, source):
        part = gathered.at[source, pl.ds(p * z.piece, z.piece)]
        return pltpu.make_async_remote_copy(
            src_ref=part,
            dst_ref=part,
            send_sem=sib_send.at[key, p],
            recv_sem=sib_recv.at[key, p],
            device_id={"row": sibling},
            device_id_type=MESH,
        )

    def to_owner(k):
        return pltpu.make_async_remote_copy(
            src_ref=packed.at[lax.rem(me + k, z.n)],
            dst_ref=left.at[me],
            send_sem=left_send.at[k],
            recv_sem=left_recv.at[k],
            device_id={"row": lax.rem(me + k, z.n)},
            device_id_type=MESH,
        )

    started = []

    def start(copy):
        copy.start()
        started.append(copy)

    def travels(direction, hop, u):
        return hop < z.hops or (hop == z.hops and u == direction)

    def send_own(wave):
        for u in range(2):
            for direction in range(2):
                if travels(direction, 1, u):
                    start(ring(direction, 1, wave * 2 + u, me))

    def send_across(wave):
        for u in range(2):
            start(across(0, wave * 2 + u, me))

    def pass_on(wave, hop):
        for u in range(2):
            for direction in range(2):
                if not travels(direction, hop, u):
                    continue
                p = wave * 2 + u
                source = device_at(place + (hop if direction else z.chips - hop))
                ring(direction, hop, p, source).wait_recv()
                if travels(direction, hop + 1, u):
                    start(ring(direction, hop + 1, p, source))
                key = hop if direction == 0 or hop == z.hops else z.hops + hop
                start(across(key, p, source))

    def wait_across(p):
        for key in range(z.chips):
            step = key if key <= z.hops else z.hops - key
            source = device_at(place - step + z.chips) + 1 - 2 * core
            across(key, p, source).wait_recv()

    for load in loads:
        load.wait()
    w1t = jnp.concatenate([w1[...]] * z.pack, axis=0)
    b1_wide = jnp.concatenate([b1[...]] * z.pack, axis=1)
    eye = lax.broadcasted_iota(jnp.int32, (z.width, z.width), 0) == lax.broadcasted_iota(
        jnp.int32, (z.width, z.width), 1
    )
    b2_tall = jnp.sum(jnp.where(eye, b2[...], 0.0), axis=1, keepdims=True)
    params = (w1t, b1_wide, w2[...], b2_tall, scale[...], shift[...])
    rows = 2 * z.piece
    for wave in range(z.waves):
        x_loads[wave].wait()
        project(z, wave, x, params, wide, tall)
        part = wide[pl.ds(wave * rows * ROWS16, rows * ROWS16), :]
        gathered[me, pl.ds(wave * rows, rows)] = part.reshape(rows, ROWS16, LANES).astype(jnp.bfloat16)
        if wave == 0:
            pl.semaphore_wait(barrier, z.n - 1)
            send_own(0)
            send_across(0)
    pack_left(z, tall, flat, packed)
    for k in range(1, z.n):
        start(to_owner(k))
    left[me] = packed[me]
    pass_on(0, 1)
    turn_weights(z, w, wide_w, wt)
    for hop in range(2, z.hops + 1):
        pass_on(0, hop)
        if hop == 2:
            for wave in range(1, z.waves):
                send_own(wave)
                send_across(wave)
    for k in range(1, z.n):
        pltpu.make_async_remote_copy(
            src_ref=packed.at[me],
            dst_ref=left.at[lax.rem(me - k + z.n, z.n)],
            send_sem=left_send.at[k],
            recv_sem=left_recv.at[k],
            device_id={"row": lax.rem(me + k, z.n)},
            device_id_type=MESH,
        ).wait_recv()
    spread_left(z, left, a)

    for wave in range(z.waves):
        pending = list(range(1, z.hops + 1)) if wave + 1 < z.waves else []
        items = z.per_wave * 4
        each = -(-len(pending) // items)
        waited = set()
        for at in range(z.per_wave):
            c = wave * z.per_wave + at
            for item in range(4):
                for hop in pending[:each]:
                    pass_on(wave + 1, hop)
                pending = pending[each:]
                u = item % 2
                if item < 2:
                    if u not in waited:
                        waited.add(u)
                        wait_across(wave * 2 + u)
                    outer_part(z, c, u, a, gathered, held)
                else:
                    map_part(z, c, u, inverse, wt, bias, held, out_ref)
    for copy in started:
        copy.wait_send()


def solution(mesh):
    n = mesh.shape["row"]
    vmem = pl.BlockSpec(memory_space=pltpu.VMEM)

    def local(x, scale, shift, w1, b1, w2, b2, w, bias):
        z = Sizes(n, x.shape[0], x.shape[1], w1.shape[1], w.shape[1])
        inverse = 1.0 / (n * x.shape[0])
        pieces = 2 * z.waves
        operands = (
            x, scale.reshape(1, -1), shift.reshape(1, -1), w1.T, b1.reshape(1, -1),
            w2.T, b2.reshape(1, -1), w, bias.reshape(1, -1),
        )
        dma = pltpu.SemaphoreType.DMA
        bf16, f32 = jnp.bfloat16, jnp.float32
        return pl.pallas_call(
            functools.partial(kernel, z, inverse),
            out_shape=jax.ShapeDtypeStruct((z.own, z.res, z.cz), bf16),
            in_specs=[pl.BlockSpec(memory_space=pl.ANY)] * 9,
            out_specs=vmem,
            scratch_shapes=[pltpu.VMEM(o.shape, o.dtype) for o in operands]
            + [
                pltpu.VMEM((z.tiles * ROWS16, LANES), f32),
                pltpu.VMEM((z.seqs * z.res, LANES), f32),
                pltpu.VMEM((n * z.q * ROWS16, LANES), f32),
                pltpu.VMEM((n, z.q, ROWS16, LANES), bf16),
                pltpu.VMEM((n, z.q, ROWS16, LANES), bf16),
                pltpu.VMEM((n, z.tiles, ROWS16, LANES), bf16),
                pltpu.VMEM(w.shape, f32),
                pltpu.VMEM((z.cz, w.shape[0]), bf16),
                pltpu.VMEM((z.parts * z.own * z.width, z.k), bf16),
                pltpu.VMEM((z.own // 2, z.width * z.width, 2 * LANES), bf16),
                dma((9 + z.waves,)),
                dma((2, z.hops, pieces)),
                dma((2, z.hops, pieces)),
                dma((z.chips, pieces)),
                dma((z.chips, pieces)),
                dma((n,)),
                dma((n,)),
            ],
            compiler_params=pltpu.CompilerParams(
                vmem_limit_bytes=56 * 2**20, collective_id=0, has_side_effects=True
            ),
        )(*operands)

    in_specs = (P(("groups", "row"), None, None), P(), P(), P(), P(), P(), P(), P(), P())
    return jax.shard_map(
        local,
        mesh=mesh,
        in_specs=in_specs,
        out_specs=P(("groups", "row"), None, None),
        check_vma=False,
    )
```

time: 80.1 us -> 41 us (0.51)
  waiting for transfers between devices: 29 us -> 0 us
  Pallas kernels: 16.5 us -> 38.5 us
  blocking collectives: 15.2 us -> 0 us
  between operations: 13.4 us -> 0.01 us
  local copies, waits for them, and re-layouts: 5.56 us -> 2.3 us
    all_gather x1 -> x0, waiting for transfers between devices: 29 us -> none  [local(): gathered = lax.all_gather(right, 'row', axis=0, tiled=False)]
    pallas_call x2 -> x1, Pallas kernels: 16.5 us -> 38.5 us  [local(): pl.pallas_call(functools.partial(kernel, z, inverse), out_shape=jax.Shape...]
    all_to_all x1 -> x0, blocking collectives: 15.2 us -> none  [local(): left = lax.all_to_all(left, 'row', split_axis=0, concat_axis=0, tiled=True)]
    unnamed x12 -> x1, local copies, waits for them, and re-layouts: 5.56 us -> 2.3 us
  transfers between devices with their start and end apart: 1 -> 0, of which waited for: 1 -> 0; matrix products, arithmetic and copies ran while one was open for 0% -> 0% of each run, Pallas kernels for 0% -> 0%
where the time goes in v2:
time: 41 us; the launch traced here: 40.8 us
  Pallas kernels  38.5 us (94%)
  local copies, waits for them, and re-layouts  2.3 us (6%)
    pallas_call x1, Pallas kernels, local(): pl.pallas_call(functools.partial(kernel, z, inverse), out_shape=jax.Shape...  38.5 us
    unnamed x1, local copies, waits for them, and re-layouts  2.3 us

profile of v2, /device:TPU:0, one launch (start us, length us, event | category | flops | bytes accessed | tf_op | source)
XLA Modules:
  0.0 40.8 jit_solution(6148318981287423712)
XLA Ops:
  0.0 38.5 %shard_map.91 = bf16[16,256,128]{2,1,0:T(8,128)(2,1)} custom-call(bf16[8,256,256]{2,1,0:T(8,128)(2,1)} %refs_0_.1, f32[1,256]{1,0:T(1,128)} %bitcast.9, f32[1,256]{1,0:T(1,128)} %bitcast.10, bf16[32,256]{1,0:T(8,128)(2,1)} %bitcast.7, f32[1,32]{1,0:T(1,128)} %bitcast.11, bf16[32,256]{1,0:T(8,128)(2,1)} %bitcast.8, f32[1,32]{1,0:T(1,128)} %bitcast.12, ...), custom_call_target="tpu_custom_call" | custom-call | tf_op jit(solution)/shard_map/pallas_call | solution.py:338
  38.5 2.3 %copy.11 = bf16[16,256,128]{2,1,0:T(8,128)(2,1)} copy(bf16[16,256,128]{2,1,0:T(8,128)(2,1)} %shard_map.91) | data formatting | bytes 2097152

commit v3 on v2

--- a/solution.py
+++ b/solution.py
@@ -31,15 +31,14 @@
         self.q = self.groups // self.ghigh
         self.k = n * ROWS16
         self.half = self.eper // 2
-        self.waves = min(2, self.chunks)
+        self.waves = 2
         self.per_wave = self.chunks // self.waves
-        self.piece = self.per_wave * self.half
+        self.piece = self.per_wave * self.eper
         self.chips = n // 2
         self.hops = self.chips // 2
 
     def tile(self, chunk, u):
-        wave, at = divmod(chunk, self.per_wave)
-        return ((wave * 2 + u) * self.per_wave + at) * self.half
+        return chunk * self.eper + u * self.half
 
 
 def project(z, wave, x_ref, params, wide, tall):
@@ -128,7 +127,7 @@
                     ]
         return carry
 
-    lax.fori_loop(0, z.half // 2, body, 0)
+    lax.fori_loop(0, z.half // 2, body, 0, unroll=True)
 
 
 def map_part(z, c, u, inverse, wt_ref, bias_ref, held, out_ref):
@@ -142,7 +141,7 @@
         return carry
 
     pairs = z.own // 2
-    lax.fori_loop(u * pairs // 2, (u + 1) * pairs // 2, body, 0)
+    lax.fori_loop(u * pairs // 2, (u + 1) * pairs // 2, body, 0, unroll=True)
 
 
 def kernel(z, inverse, *refs):
@@ -224,37 +223,34 @@
         copy.start()
         started.append(copy)
 
-    def travels(direction, hop, u):
-        return hop < z.hops or (hop == z.hops and u == direction)
+    def travels(direction, hop, wave):
+        return hop < z.hops or (hop == z.hops and wave == direction)
 
     def send_own(wave):
-        for u in range(2):
-            for direction in range(2):
-                if travels(direction, 1, u):
-                    start(ring(direction, 1, wave * 2 + u, me))
-
-    def send_across(wave):
-        for u in range(2):
-            start(across(0, wave * 2 + u, me))
+        for direction in range(2):
+            if travels(direction, 1, wave):
+                start(ring(direction, 1, wave, me))
+        start(across(0, wave, me))
 
     def pass_on(wave, hop):
-        for u in range(2):
-            for direction in range(2):
-                if not travels(direction, hop, u):
-                    continue
-                p = wave * 2 + u
-                source = device_at(place + (hop if direction else z.chips - hop))
-                ring(direction, hop, p, source).wait_recv()
-                if travels(direction, hop + 1, u):
-                    start(ring(direction, hop + 1, p, source))
-                key = hop if direction == 0 or hop == z.hops else z.hops + hop
-                start(across(key, p, source))
-
-    def wait_across(p):
+        arrived = []
+        for direction in range(2):
+            if not travels(direction, hop, wave):
+                continue
+            source = device_at(place + (hop if direction else z.chips - hop))
+            ring(direction, hop, wave, source).wait_recv()
+            if travels(direction, hop + 1, wave):
+                start(ring(direction, hop + 1, wave, source))
+            key = hop if direction == 0 or hop == z.hops else z.hops + hop
+            arrived.append(across(key, wave, source))
+        for copy in arrived:
+            start(copy)
+
+    def wait_across(wave):
         for key in range(z.chips):
             step = key if key <= z.hops else z.hops - key
             source = device_at(place - step + z.chips) + 1 - 2 * core
-            across(key, p, source).wait_recv()
+            across(key, wave, source).wait_recv()
 
     for load in loads:
         load.wait()
@@ -265,7 +261,7 @@
     )
     b2_tall = jnp.sum(jnp.where(eye, b2[...], 0.0), axis=1, keepdims=True)
     params = (w1t, b1_wide, w2[...], b2_tall, scale[...], shift[...])
-    rows = 2 * z.piece
+    rows = z.piece
     for wave in range(z.waves):
         x_loads[wave].wait()
         project(z, wave, x, params, wide, tall)
@@ -273,20 +269,17 @@
         gathered[me, pl.ds(wave * rows, rows)] = part.reshape(rows, ROWS16, LANES).astype(jnp.bfloat16)
         if wave == 0:
             pl.semaphore_wait(barrier, z.n - 1)
-            send_own(0)
-            send_across(0)
+        send_own(wave)
+    pass_on(0, 1)
     pack_left(z, tall, flat, packed)
+    pass_on(1, 1)
     for k in range(1, z.n):
         start(to_owner(k))
     left[me] = packed[me]
-    pass_on(0, 1)
     turn_weights(z, w, wide_w, wt)
-    for hop in range(2, z.hops + 1):
-        pass_on(0, hop)
-        if hop == 2:
-            for wave in range(1, z.waves):
-                send_own(wave)
-                send_across(wave)
+    for hop in range(2, z.hops):
+        for wave in range(z.waves):
+            pass_on(wave, hop)
     for k in range(1, z.n):
         pltpu.make_async_remote_copy(
             src_ref=packed.at[me],
@@ -297,26 +290,17 @@
             device_id_type=MESH,
         ).wait_recv()
     spread_left(z, left, a)
+    pass_on(0, z.hops)
+    pass_on(1, z.hops)
 
     for wave in range(z.waves):
-        pending = list(range(1, z.hops + 1)) if wave + 1 < z.waves else []
-        items = z.per_wave * 4
-        each = -(-len(pending) // items)
-        waited = set()
+        wait_across(wave)
         for at in range(z.per_wave):
             c = wave * z.per_wave + at
-            for item in range(4):
-                for hop in pending[:each]:
-                    pass_on(wave + 1, hop)
-                pending = pending[each:]
-                u = item % 2
-                if item < 2:
-                    if u not in waited:
-                        waited.add(u)
-                        wait_across(wave * 2 + u)
-                    outer_part(z, c, u, a, gathered, held)
-                else:
-                    map_part(z, c, u, inverse, wt, bias, held, out_ref)
+            for u in range(2):
+                outer_part(z, c, u, a, gathered, held)
+            for u in range(2):
+                map_part(z, c, u, inverse, wt, bias, held, out_ref)
     for copy in started:
         copy.wait_send()
 
@@ -328,17 +312,18 @@
     def local(x, scale, shift, w1, b1, w2, b2, w, bias):
         z = Sizes(n, x.shape[0], x.shape[1], w1.shape[1], w.shape[1])
         inverse = 1.0 / (n * x.shape[0])
-        pieces = 2 * z.waves
+        pieces = z.waves
         operands = (
             x, scale.reshape(1, -1), shift.reshape(1, -1), w1.T, b1.reshape(1, -1),
             w2.T, b2.reshape(1, -1), w, bias.reshape(1, -1),
         )
         dma = pltpu.SemaphoreType.DMA
+        room = 24 if z.n <= 16 else 48
         bf16, f32 = jnp.bfloat16, jnp.float32
         return pl.pallas_call(
             functools.partial(kernel, z, inverse),
             out_shape=jax.ShapeDtypeStruct((z.own, z.res, z.cz), bf16),
-            in_specs=[pl.BlockSpec(memory_space=pl.ANY)] * 9,
+            in_specs=[pl.BlockSpec(memory_space=pltpu.HBM)] * 9,
             out_specs=vmem,
             scratch_shapes=[pltpu.VMEM(o.shape, o.dtype) for o in operands]
             + [
@@ -361,7 +346,7 @@
                 dma((n,)),
             ],
             compiler_params=pltpu.CompilerParams(
-                vmem_limit_bytes=56 * 2**20, collective_id=0, has_side_effects=True
+                vmem_limit_bytes=room * 2**20, collective_id=0, has_side_effects=True
             ),
         )(*operands)
 

time: 41 us -> 33.6 us (0.82)
  Pallas kernels: 38.5 us -> 27.9 us
  local copies, waits for them, and re-layouts: 2.3 us -> 5.3 us
    pallas_call x1, Pallas kernels: 38.5 us -> 27.9 us  [local(): pl.pallas_call(functools.partial(kernel, z, inverse), out_shape=jax.Shape...]
    unnamed x1 -> x19, local copies, waits for them, and re-layouts: 2.3 us -> 5.3 us
where the time goes in v3:
time: 33.6 us; the launch traced here: 33.2 us
  Pallas kernels  27.9 us (83%)
  local copies, waits for them, and re-layouts  5.3 us (16%)
    pallas_call x1, Pallas kernels, local(): pl.pallas_call(functools.partial(kernel, z, inverse), out_shape=jax.Shape...  27.9 us
    unnamed x19, local copies, waits for them, and re-layouts  5.3 us

profile of v3, /device:TPU:0, one launch (start us, length us, event | category | flops | bytes accessed | tf_op | source)
XLA Modules:
  0.0 33.2 jit_solution(5589681238842427415)
XLA Ops:
  0.0 0.0 copy-start.5
  0.0 0.0 copy-start.7
  0.0 0.0 copy-start.8
  0.0 0.0 copy-start.4
  0.0 0.0 copy-start.6
  0.0 0.7 %copy-done.5 = f32[256]{0:T(256)S(1)} copy-done((f32[256]{0:T(256)S(1)}, f32[256]{0:T(256)}, u32[]{:S(2)}) %copy-start.5) | copy-done | bytes 1048
  0.7 0.0 copy-done.7
  0.7 0.0 copy-done.8
  0.7 0.0 copy-done.4
  0.7 0.0 copy-done.6
  0.7 0.0 copy-start
  0.7 1.2 %copy-done = bf16[8,256,256]{2,1,0:T(8,128)(2,1)S(1)} copy-done((bf16[8,256,256]{2,1,0:T(8,128)(2,1)S(1)}, bf16[8,256,256]{2,1,0:T(8,128)(2,1)}, u32[]{:S(2)}) %copy-start) | copy-done | bytes 1048600
  2.0 0.0 copy-start.1
  2.0 0.9 %copy-done.1 = bf16[1024,128]{1,0:T(8,128)(2,1)S(1)} copy-done((bf16[1024,128]{1,0:T(8,128)(2,1)S(1)}, bf16[1024,128]{1,0:T(8,128)(2,1)}, u32[]{:S(2)}) %copy-start.1) | copy-done | bytes 262168
  2.9 0.0 copy-start.2
  2.9 0.7 %copy-done.2 = bf16[256,32]{0,1:T(8,128)(2,1)S(1)} copy-done((bf16[256,32]{0,1:T(8,128)(2,1)S(1)}, bf16[256,32]{0,1:T(8,128)(2,1)}, u32[]{:S(2)}) %copy-start.2) | copy-done | bytes 16408
  3.6 0.0 copy-start.3
  3.6 0.7 %copy-done.3 = bf16[256,32]{0,1:T(8,128)(2,1)S(1)} copy-done((bf16[256,32]{0,1:T(8,128)(2,1)S(1)}, bf16[256,32]{0,1:T(8,128)(2,1)}, u32[]{:S(2)}) %copy-start.3) | copy-done | bytes 16408
  4.3 27.9 %shard_map.91 = bf16[16,256,128]{2,1,0:T(8,128)(2,1)S(1)} custom-call(bf16[8,256,256]{2,1,0:T(8,128)(2,1)S(1)} %copy-done, f32[1,256]{1,0:T(1,128)S(1)} %bitcast.9, f32[1,256]{1,0:T(1,128)S(1)} %bitcast.10, bf16[32,256]{1,0:T(8,128)(2,1)S(1)} %bitcast.7, f32[1,32]{1,0:T(1,128)S(1)} %bitcast.11, bf16[32,256]{1,0:T(8,128)(2,1)S(1)} %bitcast.8, ...), custom_call_target="tpu_custom_call" | custom-call | tf_op jit(solution)/shard_map/pallas_call | solution.py:323
  32.3 1.0 %copy.11 = bf16[16,256,128]{2,1,0:T(8,128)(2,1)} copy(bf16[16,256,128]{2,1,0:T(8,128)(2,1)S(1)} %shard_map.91) | data formatting | bytes 2097152
Async XLA Ops:
  0.0 0.7 %copy-start.5 = (f32[256]{0:T(256)S(1)}, f32[256]{0:T(256)}, u32[]{:S(2)}) copy-start(f32[256]{0:T(256)} %param.11) | copy-start | bytes 3076
  0.0 0.7 %copy-start.7 = (f32[32]{0:T(128)S(1)}, f32[32]{0:T(128)}, u32[]{:S(2)}) copy-start(f32[32]{0:T(128)} %param.15) | copy-start | bytes 388
  0.0 0.7 %copy-start.8 = (f32[128]{0:T(128)S(1)}, f32[128]{0:T(128)}, u32[]{:S(2)}) copy-start(f32[128]{0:T(128)} %param.17) | copy-start | bytes 1540
  0.0 0.7 %copy-start.4 = (f32[256]{0:T(256)S(1)}, f32[256]{0:T(256)}, u32[]{:S(2)}) copy-start(f32[256]{0:T(256)} %param.10) | copy-start | bytes 3076
  0.0 0.7 %copy-start.6 = (f32[32]{0:T(128)S(1)}, f32[32]{0:T(128)}, u32[]{:S(2)}) copy-start(f32[32]{0:T(128)} %param.13) | copy-start | bytes 388
  0.7 1.2 %copy-start = (bf16[8,256,256]{2,1,0:T(8,128)(2,1)S(1)}, bf16[8,256,256]{2,1,0:T(8,128)(2,1)}, u32[]{:S(2)}) copy-start(bf16[8,256,256]{2,1,0:T(8,128)(2,1)} %refs_0_.1) | copy-start | bytes 3145732
  2.0 0.9 %copy-start.1 = (bf16[1024,128]{1,0:T(8,128)(2,1)S(1)}, bf16[1024,128]{1,0:T(8,128)(2,1)}, u32[]{:S(2)}) copy-start(bf16[1024,128]{1,0:T(8,128)(2,1)} %refs_7_.1) | copy-start | bytes 786436
  2.9 0.7 %copy-start.2 = (bf16[256,32]{0,1:T(8,128)(2,1)S(1)}, bf16[256,32]{0,1:T(8,128)(2,1)}, u32[]{:S(2)}) copy-start(bf16[256,32]{0,1:T(8,128)(2,1)} %param.12) | copy-start | bytes 49156
  3.6 0.7 %copy-start.3 = (bf16[256,32]{0,1:T(8,128)(2,1)S(1)}, bf16[256,32]{0,1:T(8,128)(2,1)}, u32[]{:S(2)}) copy-start(bf16[256,32]{0,1:T(8,128)(2,1)} %param.14) | copy-start | bytes 49156
